TPU v7x, 512 devices: a whole 4x4x16 slice. The times are simulated.
512 devices in a mesh: aux: 64 (over y, z), fock: 8 (over x, core).
Axes of the slice: x: 4, y: 4, z: 16, core: 2. Of those that a mesh axis runs over, the one named last changes fastest.
Arguments:
- three_index: bfloat16 [512, 4096, 512], P('fock', 'aux'), may hold values from -0.25 to 0.25
- col_blocks: int32 [64, 8], replicated, may hold values from 0 to 63, as said below
- pair_mask: int32 [64, 8], replicated, may hold values 0 or 1
- occ_coef: bfloat16 [4096, 384], P('aux'), may hold values from -6 to 6
- occ_mask: int32 [64, 6], replicated, may hold values 0 or 1
- kept: int32 [128, 2], replicated, may hold values from 0 to 63, as said below
Outputs:
- exchange_blocks: float32 [128, 4096], P('fock', 'aux')
Inputs may be any that keep to these rules, and one draw needn't show every extreme that they name: `col_blocks`: each row r names 8 different column blocks; the first is r itself, the second is either (r - 1) mod 64 or (r + 32) mod 64. `kept`: each pair names two different blocks and no ordered pair repeats; every row block is the first entry of exactly 2 pairs. The pairs stand in no particular order.
All inputs are finite; a program needn't handle non-finite values.
Results may differ from a plain program's by a relative error of at most 0.0039.
Values may be sent and summed in bfloat16 or wider, within the bound.
A program may use at most 64 MiB of HBM per device.

v0:
```python
import jax
import jax.numpy as jnp
from jax import lax
from jax.sharding import PartitionSpec as P


def per_device(three_index, col_blocks, pair_mask, occ_coef, occ_mask, kept):
    fock_count = lax.axis_size("fock")
    my_index = lax.axis_index("aux")
    block_width = occ_coef.shape[0]
    occ_count = occ_coef.shape[1]
    block_count = col_blocks.shape[0]
    stored = col_blocks.shape[1]
    factor = float(three_index.shape[0] * fock_count * occ_count) ** (-0.5)
    own_mask = lax.dynamic_index_in_dim(occ_mask, my_index, 0, keepdims=False)
    own_coef = occ_coef * jnp.repeat(own_mask, block_width).astype(jnp.bfloat16)[None, :]
    whole_coef = lax.all_gather(own_coef, "aux", axis=0, tiled=True)
    coef_tiles = whole_coef.reshape(block_count, block_width, occ_count)
    col_ids = lax.dynamic_index_in_dim(col_blocks, my_index, 0, keepdims=False)
    keep_flags = lax.dynamic_index_in_dim(pair_mask, my_index, 0, keepdims=False)
    flat_slab = three_index.reshape(three_index.shape[0] * block_width, stored * block_width)
    row_tiles = coef_tiles[col_ids] * keep_flags.astype(jnp.bfloat16)[:, None, None]
    half_block = jnp.dot(
        flat_slab,
        row_tiles.reshape(stored * block_width, occ_count),
        preferred_element_type=jnp.float32,
    )
    half_block = half_block.astype(jnp.bfloat16).reshape(
        three_index.shape[0], block_width, occ_count
    )
    local_half = lax.all_to_all(half_block, "aux", split_axis=0, concat_axis=1, tiled=True)
    half_grid = local_half.reshape(local_half.shape[0], block_count, block_width, occ_count)
    left_rows = half_grid[:, kept[:, 0]]
    right_rows = half_grid[:, kept[:, 1]]
    partial_terms = (
        jnp.einsum("pkmi,pkni->kmn", left_rows, right_rows, preferred_element_type=jnp.float32)
        * factor
    )
    partial_terms = partial_terms.reshape(kept.shape[0], block_width * block_width)
    half_summed = lax.psum_scatter(partial_terms, "fock", scatter_dimension=0, tiled=True)
    return lax.psum_scatter(half_summed, "aux", scatter_dimension=1, tiled=True)


def solution(mesh):
    in_specs = (P("fock", "aux", None), P(), P(), P("aux", None), P(), P())
    out_specs = P("fock", "aux")
    return jax.shard_map(
        per_device, mesh=mesh, in_specs=in_specs, out_specs=out_specs, check_vma=False
    )
```

profile of v0, /device:TPU:1, one launch (start us, length us, event | category | flops | bytes accessed | tf_op | source)
XLA Modules:
  0.0 1064.0 jit_solution(2074476282957732460)
XLA Ops:
  6.5 0.0 copy-start
  6.5 0.0 all-gather.2.cloned.1.call-start
  6.5 0.9 fusion.1
  7.4 0.1 broadcast_in_dim.2
  7.5 0.1 convert_element_type.32
  7.6 1.4 broadcast_multiply_fusion.1
  9.0 0.0 all-gather.2.cloned.1.call-update
  9.0 0.0 copy-done
  9.0 0.2 dynamic-slice_reduce_fusion
  9.2 0.9 fusion.2
  10.1 140.7 %all-gather.2.cloned.1.call-done = bf16[4096,384]{1,0:T(8,128)(2,1)} async-done(((bf16[64,384]{1,0:T(8,128)(2,1)}), bf16[4096,384]{1,0:T(8,128)(2,1)}) %all-gather.2.cloned.1.call-update) | async-done | bytes 3145744 | tf_op jit(solution)/shard_map/all_gather | solution.py:17
  150.8 2.5 gather_fusion
  153.3 0.1 broadcast_multiply_fusion
  153.4 4.1 fusion
  157.6 2.8 copy.10
  160.4 0.0 copy-start.1
  160.4 9.1 all-to-all-start
  169.5 0.0 reduce-scatter.7.cloned.1.call-start
  169.5 0.0 copy-done.1
  169.6 129.2 %all-to-all-done = bf16[64,64,384]{2,1,0:T(8,128)(2,1)S(1)} async-done(((bf16[64,64,384]{2,1,0:T(8,128)(2,1)}), bf16[64,64,384]{2,1,0:T(8,128)(2,1)S(1)}, u32[]{:S(2)}, u32[]{:S(2)}) %all-to-all-start) | async-done | bytes 3145760 | tf_op jit(solution)/shard_map/all_to_all | solution.py:31
  298.8 4.1 gather_fusion.1
  302.8 4.1 gather_fusion.2
  306.9 8.9 convolution_multiply_fusion
  315.8 3.8 copy.11
  319.6 1.9 copy.13
  321.5 0.0 reduce-scatter.7.cloned.1.call-update
  321.5 0.0 reduce-scatter.5.cloned.1.call-start
  321.6 46.8 %reduce-scatter.7.cloned.1.call-done = f32[16,4096]{1,0:T(8,128)} async-done(((f32[128,4096]{1,0:T(8,128)}), f32[16,4096]{1,0:T(8,128)}) %reduce-scatter.7.cloned.1.call-update) | async-done | bytes 262160
  368.4 2.9 copy.14
  371.3 0.0 reduce-scatter.5.cloned.1.call-update
  371.3 684.7 %reduce-scatter.5.cloned.1.call-done = f32[16,64]{0,1:T(8,128)} async-done(((f32[16,4096]{0,1:T(8,128)}), f32[16,64]{0,1:T(8,128)}) %reduce-scatter.5.cloned.1.call-update) | async-done | bytes 4112 | tf_op jit(solution)/shard_map/reduce_scatter | solution.py:41
  1056.0 1.4 copy.12
  (4 shorter events, 0.0 us)
Async XLA Ops:
  6.5 2.5 copy-start
  6.5 144.3 %all-gather.2.cloned.1.call-start = ((), (), s32[]{:S(2)}) async-start(), calls=%async_computation.3 | async-start | bytes 3194880 | tf_op jit(solution)/shard_map/all_gather | solution.py:17
  160.4 9.2 copy-start.1
  160.4 138.4 %all-to-all-start = ((bf16[64,64,384]{2,1,0:T(8,128)(2,1)}), bf16[64,64,384]{2,1,0:T(8,128)(2,1)S(1)}, u32[]{:S(2)}, u32[]{:S(2)}) async-start(bf16[64,64,384]{2,1,0:T(8,128)(2,1)} %bitcast.20), calls=%async_computation | async-start | bytes 6291456 | tf_op jit(solution)/shard_map/all_to_all | solution.py:31
  169.5 198.9 %reduce-scatter.7.cloned.1.call-start = ((), (), s32[]{:S(2)}) async-start(), calls=%async_computation.5 | async-start | bytes 2359296
  321.5 734.5 %reduce-scatter.5.cloned.1.call-start = ((), (), s32[]{:S(2)}) async-start(), calls=%async_computation.4 | async-start | bytes 2129920 | tf_op jit(solution)/shard_map/reduce_scatter | solution.py:41
Sparse Core Ops, SparseCore 0:
  10.3 140.4 all-gather.1
  321.6 46.6 reduce-scatter.6
  372.8 683.2 reduce-scatter.4
where the time goes:
time: 1070 us; the launch traced here: 1060 us
  waiting for transfers between devices  1000 us (93%)
  local copies, waits for them, and re-layouts  23.8 us (2%)
  between operations  13.2 us (1%)
  matrix products  13 us (1%)
    reduce_scatter x1, waiting for transfers between devices, per_device(): return lax.psum_scatter(half_summed, 'aux', scatter_dimension=1, tiled=True)  685 us
    all_gather x1, waiting for transfers between devices, per_device(): whole_coef = lax.all_gather(own_coef, 'aux', axis=0, tiled=True)  141 us
    all_to_all x1, waiting for transfers between devices, per_device(): lax.all_to_all(half_block, 'aux', split_axis=0, concat_axis=1, tiled=True)  129 us
    unnamed x4, waiting for transfers between devices  46.8 us
  transfers between devices with their start and end apart: 4, of which 4 were waited for; matrix products, arithmetic and copies ran while one was open for 0% of the time, Pallas kernels for 0%

commit v1 on v0

v1 whole, which is shorter than its diff:
```python
import jax
import jax.numpy as jnp
from jax import lax
from jax.experimental import pallas as pl
from jax.experimental.pallas import tpu as pltpu
from jax.sharding import PartitionSpec as P

MESH = pl.DeviceIdType.MESH
NY, NZ, NX, NC = 4, 16, 4, 2
NAUX_DEV = NY * NZ
BS = 64
SLOTS = 8
CHUNK = 128
CHUNKS = 3


def wait_for(ref, sem):
    pltpu.make_async_copy(ref, ref, sem).wait()


def kernel(factor, three_ref, colb_ref, pmask_ref, coef_ref, omask_ref, kept_ref, out_ref,
           tri, masked, g0, g1, x0, x1, w0, w1, w2, s0, s1, s2, r0, r1, r2, kacc, cb, xs, xb, ys, yb,
           vb, zs, zb, tsem, gsend, grecv, asend, arecv, csend, crecv, tsend, trecv):
    me = lax.axis_index("aux")
    fk = lax.axis_index("fock")
    y, z = me // NZ, me % NZ
    x, c = fk // NC, fk % NC
    sib = x * NC + (1 - c)

    load = pltpu.make_async_copy(three_ref, tri, tsem)
    load.start()

    bar = pltpu.get_barrier_semaphore()

    def greet(d, carry):
        pl.semaphore_signal(bar, inc=1, device_id=((me + d) % NAUX_DEV, fk), device_id_type=MESH)
        return carry

    lax.fori_loop(1, NAUX_DEV, greet, 0)
    for dx in range(1, NX):
        pl.semaphore_signal(bar, inc=1, device_id=(me, ((x + dx) % NX) * NC + c), device_id_type=MESH)
    pl.semaphore_signal(bar, inc=1, device_id=(me, sib), device_id_type=MESH)

    lane = lax.broadcasted_iota(jnp.int32, (BS, CHUNK), 1)
    for j in range(CHUNKS):
        m_lo = omask_ref[me, 2 * j].astype(jnp.float32)
        m_hi = omask_ref[me, 2 * j + 1].astype(jnp.float32)
        keep = jnp.where(lane < BS, m_lo, m_hi)
        part = coef_ref[:, j * CHUNK:(j + 1) * CHUNK].astype(jnp.float32) * keep
        masked[j] = part.astype(jnp.bfloat16).reshape(NX, 16, CHUNK)

    pl.semaphore_wait(bar, NAUX_DEV - 1 + NX - 1 + 1)

    def z_stage(w, g, chunk):
        def send(d, carry):
            tz = (z + d) % NZ
            pltpu.make_async_remote_copy(
                src_ref=masked.at[chunk, x], dst_ref=g.at[me],
                send_sem=gsend.at[3 * w], recv_sem=grecv.at[3 * w],
                device_id=(y * NZ + tz, fk), device_id_type=MESH).start()
            return carry
        lax.fori_loop(1, NZ, send, 0)
        g[me] = masked[chunk, x]

    def y_stage(w, g):
        wait_for(g.at[pl.ds(0, NZ - 1)], grecv.at[3 * w])
        for dy in range(1, NY):
            ty = (y + dy) % NY
            rows = g.at[pl.ds(y * NZ, NZ)]
            pltpu.make_async_remote_copy(
                src_ref=rows, dst_ref=rows,
                send_sem=gsend.at[3 * w + 1], recv_sem=grecv.at[3 * w + 1],
                device_id=(ty * NZ + z, fk), device_id_type=MESH).start()

    def x_stage(w, g, xsel, wt):
        wait_for(g.at[pl.ds(0, (NY - 1) * NZ)], grecv.at[3 * w + 1])
        for s in range(SLOTS):
            flag = pmask_ref[me, s].astype(jnp.float32)
            piece = g[colb_ref[me, s]].astype(jnp.float32) * flag
            piece = piece.astype(jnp.bfloat16)
            xsel[s] = piece
            wt[s, x] = piece
        for dx in range(1, NX):
            tx = (x + dx) % NX
            pltpu.make_async_remote_copy(
                src_ref=xsel, dst_ref=wt.at[:, x],
                send_sem=gsend.at[3 * w + 2], recv_sem=grecv.at[3 * w + 2],
                device_id=(me, tx * NC + c), device_id_type=MESH).start()

    def x_wait(w, wt):
        wait_for(wt.at[:, pl.ds(0, NX - 1)], grecv.at[3 * w + 2])

    def chunk_out(o, wt, s_ref, r_ref):
        def product(tz):
            rows = tri[:, tz].reshape(NY * BS, SLOTS * BS)
            weights = wt[...].reshape(SLOTS * BS, CHUNK)
            half = jnp.dot(rows, weights, preferred_element_type=jnp.float32)
            s_ref[:, tz] = half.astype(jnp.bfloat16).reshape(NY, BS, CHUNK)

        def send(ty, tz):
            pltpu.make_async_remote_copy(
                src_ref=s_ref.at[ty, tz], dst_ref=r_ref.at[me],
                send_sem=asend.at[o], recv_sem=arecv.at[o],
                device_id=(ty * NZ + tz, fk), device_id_type=MESH).start()

        def step(q, carry):
            dz = ((q + 1) // 2) * (2 * (q % 2) - 1)
            tz = (z + dz + NZ) % NZ
            product(tz)
            for dy in range(NY):
                send((y + dy) % NY, tz)
            return carry

        lax.fori_loop(1, NZ, step, 0)
        product(z)
        for dy in range(1, NY):
            send((y + dy) % NY, z)
        r_ref[me] = s_ref[y, z]

    pair_lane = lax.broadcasted_iota(jnp.int32, (BS, 2 * BS), 1)

    def group(o, r_ref, tx, tc):
        base = (tx * NC + tc) * 16
        for j in range(8):
            lo, hi = base + j, base + 8 + j
            left = jnp.concatenate([r_ref[kept_ref[lo, 0]], r_ref[kept_ref[hi, 0]]], axis=0)
            right = jnp.concatenate([r_ref[kept_ref[lo, 1]], r_ref[kept_ref[hi, 1]]], axis=0)
            both = lax.dot_general(left, right, (((1,), (1,)), ((), ())), preferred_element_type=jnp.float32)
            pick = jnp.where(pair_lane < BS, both[:BS], both[BS:]).reshape(NY, 16, 2 * BS)
            if o == 0:
                kacc[tx, tc, j] = pick
            else:
                kacc[tx, tc, j] += pick

    z_stage(0, g0, c)
    z_stage(1, g1, 2)
    y_stage(0, g0)
    y_stage(1, g1)
    x_stage(0, g0, x0, w0)
    load.wait()
    x_wait(0, w0)
    swap = pltpu.make_async_remote_copy(
        src_ref=w0, dst_ref=w1, send_sem=gsend.at[6], recv_sem=grecv.at[6],
        device_id=(me, sib), device_id_type=MESH)
    swap.start()
    chunk_out(0, w0, s0, r0)
    x_stage(1, g1, x1, w2)
    swap.wait()
    chunk_out(1, w1, s1, r1)
    x_wait(1, w2)
    chunk_out(2, w2, s2, r2)

    for o, r_ref in ((0, r0), (1, r1)):
        wait_for(r_ref.at[pl.ds(0, NAUX_DEV - 1)], arecv.at[o])

        def all_groups(t, carry):
            group(o, r_ref, t // NC, t % NC)
            return carry

        lax.fori_loop(0, NX * NC, all_groups, 0)

    wait_for(r2.at[pl.ds(0, NAUX_DEV - 1)], arecv.at[2])

    def core_copy(tx):
        return pltpu.make_async_remote_copy(
            src_ref=kacc.at[tx, 1 - c], dst_ref=cb.at[tx],
            send_sem=csend.at[tx], recv_sem=crecv.at[tx],
            device_id=(me, sib), device_id_type=MESH)

    def theirs(d, carry):
        tx = (x + d) % NX
        group(2, r2, tx, 1 - c)
        core_copy(tx).start()
        return carry

    def ours(d, carry):
        group(2, r2, (x + d) % NX, c)
        return carry

    lax.fori_loop(1, NX + 1, theirs, 0)
    lax.fori_loop(1, NX + 1, ours, 0)

    for dx in range(1, NX + 1):
        tx = (x + dx) % NX
        core_copy(tx).wait_recv()
        xs[tx] = kacc[tx, c] + cb[tx]
        if dx < NX:
            pltpu.make_async_remote_copy(
                src_ref=xs.at[tx], dst_ref=xb.at[x], send_sem=tsend.at[0], recv_sem=trecv.at[0],
                device_id=(me, tx * NC + c), device_id_type=MESH).start()

    wait_for(xb.at[pl.ds(0, NX - 1)], trecv.at[0])
    for dy in range(1, NY + 1):
        ty = (y + dy) % NY
        total = xs[x, :, ty]
        for dx in range(1, NX):
            total += xb[(x + dx) % NX, :, ty]
        ys[ty] = total
        if dy < NY:
            pltpu.make_async_remote_copy(
                src_ref=ys.at[ty], dst_ref=yb.at[y], send_sem=tsend.at[1], recv_sem=trecv.at[1],
                device_id=(ty * NZ + z, fk), device_id_type=MESH).start()

    wait_for(yb.at[pl.ds(0, NY - 1)], trecv.at[1])
    total = ys[y]
    for dy in range(1, NY):
        total += yb[(y + dy) % NY]
    vb[...] = total
    for m in range(NZ):
        zs[m] = vb[:, m, :]

    def z_send(d, carry):
        tz = (z + d) % NZ
        pltpu.make_async_remote_copy(
            src_ref=zs.at[tz], dst_ref=zb.at[z], send_sem=tsend.at[2], recv_sem=trecv.at[2],
            device_id=(y * NZ + tz, fk), device_id_type=MESH).start()
        return carry

    lax.fori_loop(1, NZ, z_send, 0)
    zb[z] = zs[z]
    wait_for(zb.at[pl.ds(0, NZ - 1)], trecv.at[2])
    result = jnp.sum(zb[...], axis=0) * factor
    out_ref[0:8, :] = result[:, :BS]
    out_ref[8:16, :] = result[:, BS:]

    for w, g, xsel in ((0, g0, x0), (1, g1, x1)):
        wait_for(g.at[pl.ds(0, NZ - 1)], gsend.at[3 * w])
        wait_for(g.at[pl.ds(0, (NY - 1) * NZ)], gsend.at[3 * w + 1])
        for _ in range(NX - 1):
            wait_for(xsel, gsend.at[3 * w + 2])
    for o, r_ref in ((0, r0), (1, r1), (2, r2)):
        wait_for(r_ref.at[pl.ds(0, NAUX_DEV - 1)], asend.at[o])
    for tx in range(NX):
        wait_for(cb.at[tx], csend.at[tx])
    wait_for(xb.at[pl.ds(0, NX - 1)], tsend.at[0])
    wait_for(yb.at[pl.ds(0, NY - 1)], tsend.at[1])
    wait_for(zb.at[pl.ds(0, NZ - 1)], tsend.at[2])


def per_device(three_index, col_blocks, pair_mask, occ_coef, occ_mask, kept):
    fock_count = lax.axis_size("fock")
    naux, rows, width = three_index.shape
    factor = float(naux * fock_count * occ_coef.shape[1]) ** (-0.5)
    bf, f32 = jnp.bfloat16, jnp.float32
    smem = pl.BlockSpec(memory_space=pltpu.SMEM)
    vmem = pl.BlockSpec(memory_space=pltpu.VMEM)
    dma = pltpu.SemaphoreType.DMA
    g = pltpu.VMEM((NAUX_DEV, 16, CHUNK), bf)
    xsel = pltpu.VMEM((SLOTS, 16, CHUNK), bf)
    wt = pltpu.VMEM((SLOTS, NX, 16, CHUNK), bf)
    send = pltpu.VMEM((NY, NZ, BS, CHUNK), bf)
    recv = pltpu.VMEM((NAUX_DEV, BS, CHUNK), bf)
    body = lambda *refs: kernel(factor, *refs)
    return pl.pallas_call(
        body,
        out_shape=jax.ShapeDtypeStruct((16, BS), f32),
        in_specs=[pl.BlockSpec(memory_space=pl.ANY), smem, smem, vmem, smem, smem],
        out_specs=vmem,
        scratch_shapes=[
            pltpu.VMEM((NY, NZ, rows, width), bf),
            pltpu.VMEM((CHUNKS, NX, 16, CHUNK), bf),
            g, g, xsel, xsel, wt, wt, wt, send, send, send, recv, recv, recv,
            pltpu.VMEM((NX, NC, 8, NY, 16, 2 * BS), f32),
            pltpu.VMEM((NX, 8, NY, 16, 2 * BS), f32),
            pltpu.VMEM((NX, 8, NY, 16, 2 * BS), f32),
            pltpu.VMEM((NX, 8, NY, 16, 2 * BS), f32),
            pltpu.VMEM((NY, 8, 16, 2 * BS), f32),
            pltpu.VMEM((NY, 8, 16, 2 * BS), f32),
            pltpu.VMEM((8, 16, 2 * BS), f32),
            pltpu.VMEM((NZ, 8, 2 * BS), f32),
            pltpu.VMEM((NZ, 8, 2 * BS), f32),
            dma, dma((7,)), dma((7,)), dma((3,)), dma((3,)), dma((4,)), dma((4,)), dma((3,)), dma((3,)),
        ],
        compiler_params=pltpu.CompilerParams(
            collective_id=0, has_side_effects=True, vmem_limit_bytes=40 * 2**20),
        cost_estimate=pl.CostEstimate(flops=2_400_000_000, bytes_accessed=8_000_000, transcendentals=0),
    )(three_index.reshape(NY, NZ, rows, width), col_blocks, pair_mask, occ_coef, occ_mask, kept)


def solution(mesh):
    in_specs = (P("fock", "aux", None), P(), P(), P("aux", None), P(), P())
    out_specs = P("fock", "aux")
    return jax.shard_map(
        per_device, mesh=mesh, in_specs=in_specs, out_specs=out_specs, check_vma=False
    )
```

time: 1070 us -> 211 us (0.20)
  waiting for transfers between devices: 1000 us -> 0 us
  Pallas kernels: 0 us -> 202 us
  local copies, waits for them, and re-layouts: 23.8 us -> 6.68 us
  between operations: 13.2 us -> 0.02 us
  matrix products: 13 us -> 0 us
    reduce_scatter x1 -> x0, waiting for transfers between devices: 685 us -> none  [per_device(): return lax.psum_scatter(half_summed, 'aux', scatter_dimension=1, tiled=True)]
    pallas_call x0 -> x1, Pallas kernels: none -> 202 us  [per_device(): pl.pallas_call(body, out_shape=jax.ShapeDtypeStruct((16, BS), f32), in_sp...]
    all_gather x1 -> x0, waiting for transfers between devices: 141 us -> none  [per_device(): whole_coef = lax.all_gather(own_coef, 'aux', axis=0, tiled=True)]
    all_to_all x1 -> x0, waiting for transfers between devices: 129 us -> none  [per_device(): lax.all_to_all(half_block, 'aux', split_axis=0, concat_axis=1, tiled=True)]
    unnamed x4 -> x0, waiting for transfers between devices: 46.8 us -> none
    dot_general x2 -> x0, matrix products: 13 us -> none  [the longest x1 8.89 us: per_device(): jnp.einsum('pkmi,pkni->kmn', left_rows, right_rows, preferred_element_typ...]
  transfers between devices with their start and end apart: 4 -> 0, of which waited for: 4 -> 0; matrix products, arithmetic and copies ran while one was open for 0% -> 0% of each run, Pallas kernels for 0% -> 0%
where the time goes in v1:
time: 211 us; the launch traced here: 209 us
  Pallas kernels  202 us (96%)
  local copies, waits for them, and re-layouts  6.68 us (3%)
    pallas_call x1, Pallas kernels, per_device(): pl.pallas_call(body, out_shape=jax.ShapeDtypeStruct((16, BS), f32), in_sp...  202 us
    unnamed x9, local copies, waits for them, and re-layouts  6.68 us

profile of v1, /device:TPU:1, one launch (start us, length us, event | category | flops | bytes accessed | tf_op | source)
XLA Modules:
  0.0 208.7 jit_solution(3758023317706801711)
XLA Ops:
  0.0 0.8 copy.7.refs_1_
  0.8 0.8 copy.8.refs_2_
  1.5 0.8 copy.9.refs_4_
  2.3 0.8 copy.10.refs_5_
  3.1 0.0 copy-start
  3.1 2.2 %copy-done = bf16[64,64,512]{2,1,0:T(8,128)(2,1)S(1)} copy-done((bf16[64,64,512]{2,1,0:T(8,128)(2,1)S(1)}, bf16[64,64,512]{2,1,0:T(8,128)(2,1)}, u32[]{:S(2)}) %copy-start) | copy-done | bytes 4194328
  5.3 0.0 copy-start.1
  5.3 0.8 copy-done.1
  6.1 202.0 %shard_map.64 = f32[16,64]{1,0:T(8,128)S(1)} custom-call(bf16[4,16,64,512]{3,2,1,0:T(8,128)(2,1)S(1)} %bitcast.1, s32[64,8]{1,0:T(8,128)S(1)} %copy.7.refs_1_, s32[64,8]{1,0:T(8,128)S(1)} %copy.8.refs_2_, bf16[64,384]{1,0:T(8,128)(2,1)S(1)} %copy-done.1, s32[64,6]{1,0:T(8,128)S(1)} %copy.9.refs_4_, s32[128,2]{1,0:T(8,128)S(1)} %copy.10.refs_5_), custom_call_target="tpu_custom_call" | custom-call | flops 2400000000 | bytes 8000000 | tf_op jit(solution)/shard_map/pallas_call | solution.py:254
  208.1 0.6 copy.12
Async XLA Ops:
  3.1 2.2 %copy-start = (bf16[64,64,512]{2,1,0:T(8,128)(2,1)S(1)}, bf16[64,64,512]{2,1,0:T(8,128)(2,1)}, u32[]{:S(2)}) copy-start(bf16[64,64,512]{2,1,0:T(8,128)(2,1)} %param.6) | copy-start | bytes 12582916
  5.3 0.8 copy-start.1

commit v2 on v1

v2 whole, which is shorter than its diff:
```python
import jax
import jax.numpy as jnp
from jax import lax
from jax.experimental import pallas as pl
from jax.experimental.pallas import tpu as pltpu
from jax.sharding import PartitionSpec as P

MESH = pl.DeviceIdType.MESH
NY, NZ, NX, NC = 4, 16, 4, 2
NAUX_DEV = NY * NZ
BS = 64
SLOTS = 8
CHUNK = 128
CHUNKS = 3


def wait_for(ref, sem):
    pltpu.make_async_copy(ref, ref, sem).wait()


def kernel(factor, three_ref, colb_ref, pmask_ref, coef_ref, omask_ref, kept_ref, out_ref,
           tri, masked, g0, g1, ysel0, ysel1, yrec0, yrec1, x0, x1, w0, w1, w2, s0, s1, s2, r0, r1, r2,
           kacc, cb, xs, xb, ys, yb, early, kst, cb2, a1s, a1r, b1s, b1r, a2s, a2r, b2s, b2r, vb, zs, zb,
           tsem, gsend, grecv, asend, arecv, csend, crecv, c2send, c2recv, tsend, trecv):
    me = lax.axis_index("aux")
    fk = lax.axis_index("fock")
    y, z = me // NZ, me % NZ
    x, c = fk // NC, fk % NC
    sib = x * NC + (1 - c)

    load = pltpu.make_async_copy(three_ref, tri, tsem)
    load.start()

    bar = pltpu.get_barrier_semaphore()

    def greet(d, carry):
        pl.semaphore_signal(bar, inc=1, device_id=(y * NZ + (z + d) % NZ, fk), device_id_type=MESH)
        return carry

    lax.fori_loop(1, NZ, greet, 0)
    for dy in range(1, NY):
        pl.semaphore_signal(bar, inc=1, device_id=(((y + dy) % NY) * NZ + z, fk), device_id_type=MESH)
    for dx in range(1, NX):
        pl.semaphore_signal(bar, inc=1, device_id=(me, ((x + dx) % NX) * NC + c), device_id_type=MESH)
    pl.semaphore_signal(bar, inc=1, device_id=(me, sib), device_id_type=MESH)

    lane = lax.broadcasted_iota(jnp.int32, (BS, CHUNK), 1)
    for j in range(CHUNKS):
        m_lo = omask_ref[2 * j, me].astype(jnp.float32)
        m_hi = omask_ref[2 * j + 1, me].astype(jnp.float32)
        keep = jnp.where(lane < BS, m_lo, m_hi)
        part = coef_ref[:, j * CHUNK:(j + 1) * CHUNK].astype(jnp.float32) * keep
        masked[j] = part.astype(jnp.bfloat16).reshape(NX, 16, CHUNK)

    pl.semaphore_wait(bar, NZ - 1 + NY - 1 + NX - 1 + 1)

    def z_stage(w, g, chunk):
        def send(d, carry):
            tz = (z + d) % NZ
            pltpu.make_async_remote_copy(
                src_ref=masked.at[chunk, x], dst_ref=g.at[z],
                send_sem=gsend.at[3 * w], recv_sem=grecv.at[3 * w],
                device_id=(y * NZ + tz, fk), device_id_type=MESH).start()
            return carry
        lax.fori_loop(1, NZ, send, 0)
        g[z] = masked[chunk, x]

    def y_stage(w, g, ysel, yrec):
        wait_for(g.at[pl.ds(0, NZ - 1)], grecv.at[3 * w])
        for dy in range(1, NY + 1):
            ty = (y + dy) % NY
            for s in range(SLOTS):
                col = colb_ref[s, ty * NZ + z]
                here = jnp.where(col // NZ == y, pmask_ref[s, ty * NZ + z], 0).astype(jnp.float32)
                piece = (g[col % NZ].astype(jnp.float32) * here).astype(jnp.bfloat16)
                if dy < NY:
                    ysel[ty, s] = piece
                else:
                    yrec[y, s] = piece
            if dy < NY:
                pltpu.make_async_remote_copy(
                    src_ref=ysel.at[ty], dst_ref=yrec.at[y],
                    send_sem=gsend.at[3 * w + 1], recv_sem=grecv.at[3 * w + 1],
                    device_id=(ty * NZ + z, fk), device_id_type=MESH).start()

    def x_stage(w, yrec, xsel, wt):
        wait_for(yrec.at[pl.ds(0, NY - 1)], grecv.at[3 * w + 1])
        piece = yrec[0].astype(jnp.float32)
        for sy in range(1, NY):
            piece += yrec[sy].astype(jnp.float32)
        piece = piece.astype(jnp.bfloat16)
        xsel[...] = piece
        wt[:, x] = piece
        for dx in range(1, NX):
            tx = (x + dx) % NX
            pltpu.make_async_remote_copy(
                src_ref=xsel, dst_ref=wt.at[:, x],
                send_sem=gsend.at[3 * w + 2], recv_sem=grecv.at[3 * w + 2],
                device_id=(me, tx * NC + c), device_id_type=MESH).start()

    def x_wait(w, wt):
        wait_for(wt.at[:, pl.ds(0, NX - 1)], grecv.at[3 * w + 2])

    def chunk_out(o, wt, s_ref, r_ref):
        def product(tz):
            rows = tri[:, tz].reshape(NY * BS, SLOTS * BS)
            weights = wt[...].reshape(SLOTS * BS, CHUNK)
            half = jnp.dot(rows, weights, preferred_element_type=jnp.float32)
            s_ref[:, tz] = half.astype(jnp.bfloat16).reshape(NY, BS, CHUNK)

        def send(ty, tz):
            pltpu.make_async_remote_copy(
                src_ref=s_ref.at[ty, tz], dst_ref=r_ref.at[me],
                send_sem=asend.at[o], recv_sem=arecv.at[o],
                device_id=(ty * NZ + tz, fk), device_id_type=MESH).start()

        def step(q, carry):
            dz = ((q + 1) // 2) * (2 * (q % 2) - 1)
            tz = (z + dz + NZ) % NZ
            product(tz)
            for dy in range(NY):
                send((y + dy) % NY, tz)
            return carry

        lax.fori_loop(1, NZ, step, 0)
        product(z)
        for dy in range(1, NY):
            send((y + dy) % NY, z)
        r_ref[me] = s_ref[y, z]

    pair_lane = lax.broadcasted_iota(jnp.int32, (BS, 2 * BS), 1)

    def group(r_ref, tx, tc, store):
        base = (tx * NC + tc) * 16
        for j in range(8):
            lo, hi = base + j, base + 8 + j
            left = jnp.concatenate([r_ref[kept_ref[0, lo]], r_ref[kept_ref[0, hi]]], axis=0)
            right = jnp.concatenate([r_ref[kept_ref[1, lo]], r_ref[kept_ref[1, hi]]], axis=0)
            both = lax.dot_general(left, right, (((1,), (1,)), ((), ())), preferred_element_type=jnp.float32)
            store(j, jnp.where(pair_lane < BS, both[:BS], both[BS:]).reshape(NY, 16, 2 * BS))

    z_stage(0, g0, c)
    z_stage(1, g1, 2)
    y_stage(0, g0, ysel0, yrec0)
    y_stage(1, g1, ysel1, yrec1)
    x_stage(0, yrec0, x0, w0)
    load.wait()
    x_wait(0, w0)
    swap = pltpu.make_async_remote_copy(
        src_ref=w0, dst_ref=w1, send_sem=gsend.at[6], recv_sem=grecv.at[6],
        device_id=(me, sib), device_id_type=MESH)
    swap.start()
    chunk_out(0, w0, s0, r0)
    x_stage(1, yrec1, x1, w2)
    swap.wait()
    chunk_out(1, w1, s1, r1)
    x_wait(1, w2)
    chunk_out(2, w2, s2, r2)

    for o, r_ref in ((0, r0), (1, r1)):
        wait_for(r_ref.at[pl.ds(0, NAUX_DEV - 1)], arecv.at[o])

        def all_groups(t, carry):
            tx, tc = t // NC, t % NC

            def store(j, pick):
                if o == 0:
                    kacc[tx, tc, j] = pick
                else:
                    kacc[tx, tc, j] += pick

            group(r_ref, tx, tc, store)
            return carry

        lax.fori_loop(0, NX * NC, all_groups, 0)

    def core_copy(tx):
        return pltpu.make_async_remote_copy(
            src_ref=kacc.at[tx, 1 - c], dst_ref=cb.at[tx],
            send_sem=csend.at[tx], recv_sem=crecv.at[tx],
            device_id=(me, sib), device_id_type=MESH)

    for dx in range(1, NX + 1):
        core_copy((x + dx) % NX).start()
    for dx in range(1, NX + 1):
        tx = (x + dx) % NX
        core_copy(tx).wait_recv()
        xs[tx] = kacc[tx, c] + cb[tx]
        if dx < NX:
            pltpu.make_async_remote_copy(
                src_ref=xs.at[tx], dst_ref=xb.at[x], send_sem=tsend.at[0], recv_sem=trecv.at[0],
                device_id=(me, tx * NC + c), device_id_type=MESH).start()

    wait_for(xb.at[pl.ds(0, NX - 1)], trecv.at[0])
    for dy in range(1, NY + 1):
        ty = (y + dy) % NY
        total = xs[x, :, ty]
        for dx in range(1, NX):
            total += xb[(x + dx) % NX, :, ty]
        ys[ty] = total
        if dy < NY:
            pltpu.make_async_remote_copy(
                src_ref=ys.at[ty], dst_ref=yb.at[y], send_sem=tsend.at[1], recv_sem=trecv.at[1],
                device_id=(ty * NZ + z, fk), device_id_type=MESH).start()

    wait_for(yb.at[pl.ds(0, NY - 1)], trecv.at[1])
    total = ys[y]
    for dy in range(1, NY):
        total += yb[(y + dy) % NY]
    early[...] = total
    for tx in range(NX):
        wait_for(cb.at[tx], csend.at[tx])

    wait_for(r2.at[pl.ds(0, NAUX_DEV - 1)], arecv.at[2])

    def core_copy2(tx):
        return pltpu.make_async_remote_copy(
            src_ref=kst.at[tx], dst_ref=cb2.at[tx],
            send_sem=c2send.at[tx], recv_sem=c2recv.at[tx],
            device_id=(me, sib), device_id_type=MESH)

    def theirs(d, carry):
        tx = (x + d) % NX

        def store(j, pick):
            kst[tx, j] = pick.astype(jnp.bfloat16)

        group(r2, tx, 1 - c, store)
        core_copy2(tx).start()
        return carry

    lax.fori_loop(1, NX + 1, theirs, 0)

    def ours(tx):
        def store(j, pick):
            kacc[tx, c, j] = pick

        group(r2, tx, c, store)
        core_copy2(tx).wait_recv()
        for half in range(2):
            pick = kacc[tx, c, half * 4:half * 4 + 4] + cb2[tx, half * 4:half * 4 + 4].astype(jnp.float32)
            pick = pick.astype(jnp.bfloat16)
            if half == 0:
                a1s[tx] = pick
            else:
                for ty in range(NY):
                    b1s[ty, tx] = pick[:, ty]

    def send_y(tx):
        for dy in range(1, NY):
            ty = (y + dy) % NY
            pltpu.make_async_remote_copy(
                src_ref=b1s.at[ty, tx], dst_ref=b1r.at[y, tx], send_sem=tsend.at[3], recv_sem=trecv.at[3],
                device_id=(ty * NZ + z, fk), device_id_type=MESH).start()

    def ours_step(d, carry):
        tx = (x + d) % NX
        ours(tx)
        pltpu.make_async_remote_copy(
            src_ref=a1s.at[tx], dst_ref=a1r.at[x], send_sem=tsend.at[2], recv_sem=trecv.at[2],
            device_id=(me, tx * NC + c), device_id_type=MESH).start()
        send_y(tx)
        return carry

    lax.fori_loop(1, NX, ours_step, 0)
    ours(x)
    send_y(x)

    wait_for(a1r.at[pl.ds(0, NX - 1)], trecv.at[2])
    for dy in range(1, NY + 1):
        ty = (y + dy) % NY
        total = a1s[x, :, ty].astype(jnp.float32)
        for dx in range(1, NX):
            total += a1r[(x + dx) % NX, :, ty].astype(jnp.float32)
        if dy < NY:
            a2s[ty] = total.astype(jnp.bfloat16)
            pltpu.make_async_remote_copy(
                src_ref=a2s.at[ty], dst_ref=a2r.at[y], send_sem=tsend.at[4], recv_sem=trecv.at[4],
                device_id=(ty * NZ + z, fk), device_id_type=MESH).start()
        else:
            vb[0:4] = total + early[0:4]

    wait_for(b1r.at[pl.ds(0, NY - 1)], trecv.at[3])
    for dx in range(1, NX + 1):
        tx = (x + dx) % NX
        total = b1s[y, tx].astype(jnp.float32)
        for dy in range(1, NY):
            total += b1r[(y + dy) % NY, tx].astype(jnp.float32)
        if dx < NX:
            b2s[tx] = total.astype(jnp.bfloat16)
            pltpu.make_async_remote_copy(
                src_ref=b2s.at[tx], dst_ref=b2r.at[x], send_sem=tsend.at[5], recv_sem=trecv.at[5],
                device_id=(me, tx * NC + c), device_id_type=MESH).start()
        else:
            vb[4:8] = total + early[4:8]

    wait_for(a2r.at[pl.ds(0, NY - 1)], trecv.at[4])
    total = vb[0:4]
    for dy in range(1, NY):
        total += a2r[(y + dy) % NY].astype(jnp.float32)
    vb[0:4] = total
    wait_for(b2r.at[pl.ds(0, NX - 1)], trecv.at[5])
    total = vb[4:8]
    for dx in range(1, NX):
        total += b2r[(x + dx) % NX].astype(jnp.float32)
    vb[4:8] = total
    for m in range(NZ):
        zs[m] = vb[:, m, :]

    def z_send(d, carry):
        tz = (z + d) % NZ
        pltpu.make_async_remote_copy(
            src_ref=zs.at[tz], dst_ref=zb.at[z], send_sem=tsend.at[6], recv_sem=trecv.at[6],
            device_id=(y * NZ + tz, fk), device_id_type=MESH).start()
        return carry

    lax.fori_loop(1, NZ, z_send, 0)
    zb[z] = zs[z]
    wait_for(zb.at[pl.ds(0, NZ - 1)], trecv.at[6])
    result = jnp.sum(zb[...], axis=0) * factor
    out_ref[0:8, :] = result[:, :BS]
    out_ref[8:16, :] = result[:, BS:]

    for w, g, yrec, xsel in ((0, g0, yrec0, x0), (1, g1, yrec1, x1)):
        wait_for(g.at[pl.ds(0, NZ - 1)], gsend.at[3 * w])
        wait_for(yrec.at[pl.ds(0, NY - 1)], gsend.at[3 * w + 1])
        for _ in range(NX - 1):
            wait_for(xsel, gsend.at[3 * w + 2])
    for o, r_ref in ((0, r0), (1, r1), (2, r2)):
        wait_for(r_ref.at[pl.ds(0, NAUX_DEV - 1)], asend.at[o])
    for tx in range(NX):
        wait_for(cb2.at[tx], c2send.at[tx])
    wait_for(xb.at[pl.ds(0, NX - 1)], tsend.at[0])
    wait_for(yb.at[pl.ds(0, NY - 1)], tsend.at[1])
    wait_for(a1r.at[pl.ds(0, NX - 1)], tsend.at[2])
    wait_for(b1r.at[pl.ds(0, NY - 1)], tsend.at[3])
    wait_for(a2r.at[pl.ds(0, NY - 1)], tsend.at[4])
    wait_for(b2r.at[pl.ds(0, NX - 1)], tsend.at[5])
    wait_for(zb.at[pl.ds(0, NZ - 1)], tsend.at[6])


def per_device(three_index, col_blocks, pair_mask, occ_coef, occ_mask, kept):
    fock_count = lax.axis_size("fock")
    naux, rows, width = three_index.shape
    factor = float(naux * fock_count * occ_coef.shape[1]) ** (-0.5)
    bf, f32 = jnp.bfloat16, jnp.float32
    smem = pl.BlockSpec(memory_space=pltpu.SMEM)
    vmem = pl.BlockSpec(memory_space=pltpu.VMEM)
    dma = pltpu.SemaphoreType.DMA
    g = pltpu.VMEM((NZ, 16, CHUNK), bf)
    ysel = pltpu.VMEM((NY, SLOTS, 16, CHUNK), bf)
    xsel = pltpu.VMEM((SLOTS, 16, CHUNK), bf)
    wt = pltpu.VMEM((SLOTS, NX, 16, CHUNK), bf)
    send = pltpu.VMEM((NY, NZ, BS, CHUNK), bf)
    recv = pltpu.VMEM((NAUX_DEV, BS, CHUNK), bf)
    first = pltpu.VMEM((4, 4, 4, 16, 2 * BS), bf)
    second = pltpu.VMEM((4, 4, 16, 2 * BS), bf)
    body = lambda *refs: kernel(factor, *refs)
    return pl.pallas_call(
        body,
        out_shape=jax.ShapeDtypeStruct((16, BS), f32),
        in_specs=[pl.BlockSpec(memory_space=pl.ANY), smem, smem, vmem, smem, smem],
        out_specs=vmem,
        scratch_shapes=[
            pltpu.VMEM((NY, NZ, rows, width), bf),
            pltpu.VMEM((CHUNKS, NX, 16, CHUNK), bf),
            g, g, ysel, ysel, ysel, ysel, xsel, xsel, wt, wt, wt, send, send, send, recv, recv, recv,
            pltpu.VMEM((NX, NC, 8, NY, 16, 2 * BS), f32),
            pltpu.VMEM((NX, 8, NY, 16, 2 * BS), f32),
            pltpu.VMEM((NX, 8, NY, 16, 2 * BS), f32),
            pltpu.VMEM((NX, 8, NY, 16, 2 * BS), f32),
            pltpu.VMEM((NY, 8, 16, 2 * BS), f32),
            pltpu.VMEM((NY, 8, 16, 2 * BS), f32),
            pltpu.VMEM((8, 16, 2 * BS), f32),
            pltpu.VMEM((NX, 8, NY, 16, 2 * BS), bf),
            pltpu.VMEM((NX, 8, NY, 16, 2 * BS), bf),
            first, first, first, first, second, second, second, second,
            pltpu.VMEM((8, 16, 2 * BS), f32),
            pltpu.VMEM((NZ, 8, 2 * BS), f32),
            pltpu.VMEM((NZ, 8, 2 * BS), f32),
            dma, dma((7,)), dma((7,)), dma((3,)), dma((3,)), dma((4,)), dma((4,)), dma((4,)), dma((4,)),
            dma((7,)), dma((7,)),
        ],
        compiler_params=pltpu.CompilerParams(
            collective_id=0, has_side_effects=True, vmem_limit_bytes=62 * 2**20),
        cost_estimate=pl.CostEstimate(flops=2_400_000_000, bytes_accessed=8_000_000, transcendentals=0),
    )(three_index.reshape(NY, NZ, rows, width), col_blocks.T, pair_mask.T, occ_coef, occ_mask.T, kept.T)


def solution(mesh):
    in_specs = (P("fock", "aux", None), P(), P(), P("aux", None), P(), P())
    out_specs = P("fock", "aux")
    return jax.shard_map(
        per_device, mesh=mesh, in_specs=in_specs, out_specs=out_specs, check_vma=False
    )
```

time: 211 us -> 192 us (0.910)
  Pallas kernels: 202 us -> 190 us
  local copies, waits for them, and re-layouts: 6.68 us -> 1.3 us
    pallas_call x1, Pallas kernels: 202 us -> 190 us  [per_device(): pl.pallas_call(body, out_shape=jax.ShapeDtypeStruct((16, BS), f32), in_sp...]
    unnamed x9 -> x1, local copies, waits for them, and re-layouts: 6.68 us -> 1.3 us
where the time goes in v2:
time: 192 us
  Pallas kernels  190 us (99%)
    pallas_call x1, Pallas kernels, per_device(): pl.pallas_call(body, out_shape=jax.ShapeDtypeStruct((16, BS), f32), in_sp...  190 us

profile of v2, /device:TPU:1, one launch (start us, length us, event | category | flops | bytes accessed | tf_op | source)
XLA Modules:
  0.0 191.6 jit_solution(15826844454564188243)
XLA Ops:
  0.0 190.3 %shard_map.64 = f32[16,64]{1,0:T(8,128)} custom-call(bf16[4,16,64,512]{3,2,1,0:T(8,128)(2,1)} %bitcast.5, s32[8,64]{1,0:T(8,128)} %bitcast.6, s32[8,64]{1,0:T(8,128)} %bitcast.7, bf16[64,384]{1,0:T(8,128)(2,1)} %refs_3_.1, s32[6,64]{1,0:T(8,128)} %bitcast.8, s32[2,128]{1,0:T(2,128)} %bitcast.9), custom_call_target="tpu_custom_call" | custom-call | flops 2400000000 | bytes 8000000 | tf_op jit(solution)/shard_map/pallas_call | solution.py:359
  190.3 1.3 copy.8

commit v3 on v2

--- a/solution.py
+++ b/solution.py
@@ -18,8 +18,8 @@
     pltpu.make_async_copy(ref, ref, sem).wait()
 
 
-def kernel(factor, three_ref, colb_ref, pmask_ref, coef_ref, omask_ref, kept_ref, out_ref,
-           tri, masked, g0, g1, ysel0, ysel1, yrec0, yrec1, x0, x1, w0, w1, w2, s0, s1, s2, r0, r1, r2,
+def kernel(factor, three_ref, colb_hbm, pmask_hbm, coef_hbm, omask_hbm, kept_hbm, out_ref,
+           colb_ref, pmask_ref, coef_ref, omask_ref, kept_ref, isem, tri, masked, g0, g1, ysel0, ysel1, yrec0, yrec1, x0, x1, w0, w1, w2, w3, s0, s1, s2, r0, r1, r2,
            kacc, cb, xs, xb, ys, yb, early, kst, cb2, a1s, a1r, b1s, b1r, a2s, a2r, b2s, b2r, vb, zs, zb,
            tsem, gsend, grecv, asend, arecv, csend, crecv, c2send, c2recv, tsend, trecv):
     me = lax.axis_index("aux")
@@ -28,13 +28,25 @@
     x, c = fk // NC, fk % NC
     sib = x * NC + (1 - c)
 
-    load = pltpu.make_async_copy(three_ref, tri, tsem)
-    load.start()
+    def away(q):
+        return (z + ((q + 1) // 2) * (2 * (q % 2) - 1) + NZ) % NZ
+
+    def far_first(q):
+        return away(NZ - q)
+
+    loads = [
+        pltpu.make_async_copy(src, dst, isem.at[k])
+        for k, (src, dst) in enumerate((
+            (omask_hbm, omask_ref), (coef_hbm, coef_ref), (colb_hbm, colb_ref),
+            (pmask_hbm, pmask_ref), (kept_hbm, kept_ref)))
+    ]
+    for copy in loads:
+        copy.start()
 
     bar = pltpu.get_barrier_semaphore()
 
     def greet(d, carry):
-        pl.semaphore_signal(bar, inc=1, device_id=(y * NZ + (z + d) % NZ, fk), device_id_type=MESH)
+        pl.semaphore_signal(bar, inc=1, device_id=(y * NZ + far_first(d), fk), device_id_type=MESH)
         return carry
 
     lax.fori_loop(1, NZ, greet, 0)
@@ -43,6 +55,11 @@
     for dx in range(1, NX):
         pl.semaphore_signal(bar, inc=1, device_id=(me, ((x + dx) % NX) * NC + c), device_id_type=MESH)
     pl.semaphore_signal(bar, inc=1, device_id=(me, sib), device_id_type=MESH)
+
+    load = pltpu.make_async_copy(three_ref, tri, tsem)
+    load.start()
+    for copy in loads:
+        copy.wait()
 
     lane = lax.broadcasted_iota(jnp.int32, (BS, CHUNK), 1)
     for j in range(CHUNKS):
@@ -54,25 +71,27 @@
 
     pl.semaphore_wait(bar, NZ - 1 + NY - 1 + NX - 1 + 1)
 
-    def z_stage(w, g, chunk):
+    def z_send_coef(w, g, chunk, slot):
         def send(d, carry):
-            tz = (z + d) % NZ
-            pltpu.make_async_remote_copy(
-                src_ref=masked.at[chunk, x], dst_ref=g.at[z],
+            tz = far_first(d)
+            pltpu.make_async_remote_copy(
+                src_ref=masked.at[chunk, x], dst_ref=g.at[slot],
                 send_sem=gsend.at[3 * w], recv_sem=grecv.at[3 * w],
                 device_id=(y * NZ + tz, fk), device_id_type=MESH).start()
             return carry
         lax.fori_loop(1, NZ, send, 0)
-        g[z] = masked[chunk, x]
+        g[slot] = masked[chunk, x]
 
     def y_stage(w, g, ysel, yrec):
-        wait_for(g.at[pl.ds(0, NZ - 1)], grecv.at[3 * w])
-        for dy in range(1, NY + 1):
+        for dy in (2, 1, 3, NY):
             ty = (y + dy) % NY
             for s in range(SLOTS):
                 col = colb_ref[s, ty * NZ + z]
-                here = jnp.where(col // NZ == y, pmask_ref[s, ty * NZ + z], 0).astype(jnp.float32)
-                piece = (g[col % NZ].astype(jnp.float32) * here).astype(jnp.bfloat16)
+                flag = pmask_ref[s, ty * NZ + z]
+                if w == 1:
+                    flag = jnp.where(col % 2 == c, flag, 0)
+                here = jnp.where(col // NZ == y, flag, 0).astype(jnp.float32).astype(jnp.bfloat16)
+                piece = g[col % NZ // (1 + w)] * here
                 if dy < NY:
                     ysel[ty, s] = piece
                 else:
@@ -91,7 +110,7 @@
         piece = piece.astype(jnp.bfloat16)
         xsel[...] = piece
         wt[:, x] = piece
-        for dx in range(1, NX):
+        for dx in (2, 1, 3):
             tx = (x + dx) % NX
             pltpu.make_async_remote_copy(
                 src_ref=xsel, dst_ref=wt.at[:, x],
@@ -115,8 +134,7 @@
                 device_id=(ty * NZ + tz, fk), device_id_type=MESH).start()
 
         def step(q, carry):
-            dz = ((q + 1) // 2) * (2 * (q % 2) - 1)
-            tz = (z + dz + NZ) % NZ
+            tz = far_first(q) if o == 2 else away(q)
             product(tz)
             for dy in range(NY):
                 send((y + dy) % NY, tz)
@@ -139,11 +157,26 @@
             both = lax.dot_general(left, right, (((1,), (1,)), ((), ())), preferred_element_type=jnp.float32)
             store(j, jnp.where(pair_lane < BS, both[:BS], both[BS:]).reshape(NY, 16, 2 * BS))
 
-    z_stage(0, g0, c)
-    z_stage(1, g1, 2)
+    mine = z % 2 == c
+    z_send_coef(0, g0, c, z)
+
+    @pl.when(mine)
+    def _():
+        z_send_coef(1, g1, 2, z // 2)
+
+    wait_for(g0.at[pl.ds(0, NZ - 1)], grecv.at[0])
     y_stage(0, g0, ysel0, yrec0)
+    x_stage(0, yrec0, x0, w0)
+
+    @pl.when(mine)
+    def _():
+        wait_for(g1.at[pl.ds(0, NZ // 2 - 1)], grecv.at[3])
+
+    @pl.when(jnp.logical_not(mine))
+    def _():
+        wait_for(g1, grecv.at[3])
+
     y_stage(1, g1, ysel1, yrec1)
-    x_stage(0, yrec0, x0, w0)
     load.wait()
     x_wait(0, w0)
     swap = pltpu.make_async_remote_copy(
@@ -155,6 +188,12 @@
     swap.wait()
     chunk_out(1, w1, s1, r1)
     x_wait(1, w2)
+    merge = pltpu.make_async_remote_copy(
+        src_ref=w2, dst_ref=w3, send_sem=gsend.at[7], recv_sem=grecv.at[7],
+        device_id=(me, sib), device_id_type=MESH)
+    merge.start()
+    merge.wait()
+    w2[...] = (w2[...].astype(jnp.float32) + w3[...].astype(jnp.float32)).astype(jnp.bfloat16)
     chunk_out(2, w2, s2, r2)
 
     for o, r_ref in ((0, r0), (1, r1)):
@@ -219,17 +258,12 @@
             send_sem=c2send.at[tx], recv_sem=c2recv.at[tx],
             device_id=(me, sib), device_id_type=MESH)
 
-    def theirs(d, carry):
-        tx = (x + d) % NX
-
+    def theirs(tx):
         def store(j, pick):
             kst[tx, j] = pick.astype(jnp.bfloat16)
 
         group(r2, tx, 1 - c, store)
         core_copy2(tx).start()
-        return carry
-
-    lax.fori_loop(1, NX + 1, theirs, 0)
 
     def ours(tx):
         def store(j, pick):
@@ -247,14 +281,15 @@
                     b1s[ty, tx] = pick[:, ty]
 
     def send_y(tx):
-        for dy in range(1, NY):
+        for dy in (2, 1, 3):
             ty = (y + dy) % NY
             pltpu.make_async_remote_copy(
                 src_ref=b1s.at[ty, tx], dst_ref=b1r.at[y, tx], send_sem=tsend.at[3], recv_sem=trecv.at[3],
                 device_id=(ty * NZ + z, fk), device_id_type=MESH).start()
 
-    def ours_step(d, carry):
-        tx = (x + d) % NX
+    def both_step(d, carry):
+        theirs((x + NX - 1 - d) % NX)
+        tx = (x + NX - d) % NX
         ours(tx)
         pltpu.make_async_remote_copy(
             src_ref=a1s.at[tx], dst_ref=a1r.at[x], send_sem=tsend.at[2], recv_sem=trecv.at[2],
@@ -262,12 +297,13 @@
         send_y(tx)
         return carry
 
-    lax.fori_loop(1, NX, ours_step, 0)
+    theirs((x + NX - 1) % NX)
+    lax.fori_loop(1, NX, both_step, 0)
     ours(x)
     send_y(x)
 
     wait_for(a1r.at[pl.ds(0, NX - 1)], trecv.at[2])
-    for dy in range(1, NY + 1):
+    for dy in (2, 1, 3, NY):
         ty = (y + dy) % NY
         total = a1s[x, :, ty].astype(jnp.float32)
         for dx in range(1, NX):
@@ -281,7 +317,7 @@
             vb[0:4] = total + early[0:4]
 
     wait_for(b1r.at[pl.ds(0, NY - 1)], trecv.at[3])
-    for dx in range(1, NX + 1):
+    for dx in (2, 1, 3, NX):
         tx = (x + dx) % NX
         total = b1s[y, tx].astype(jnp.float32)
         for dy in range(1, NY):
@@ -308,7 +344,7 @@
         zs[m] = vb[:, m, :]
 
     def z_send(d, carry):
-        tz = (z + d) % NZ
+        tz = far_first(d)
         pltpu.make_async_remote_copy(
             src_ref=zs.at[tz], dst_ref=zb.at[z], send_sem=tsend.at[6], recv_sem=trecv.at[6],
             device_id=(y * NZ + tz, fk), device_id_type=MESH).start()
@@ -321,8 +357,14 @@
     out_ref[0:8, :] = result[:, :BS]
     out_ref[8:16, :] = result[:, BS:]
 
-    for w, g, yrec, xsel in ((0, g0, yrec0, x0), (1, g1, yrec1, x1)):
-        wait_for(g.at[pl.ds(0, NZ - 1)], gsend.at[3 * w])
+    wait_for(g0.at[pl.ds(0, NZ - 1)], gsend.at[0])
+
+    @pl.when(mine)
+    def _():
+        for rows in (NZ // 2, NZ // 2 - 1):
+            wait_for(g1.at[pl.ds(0, rows)], gsend.at[3])
+
+    for w, yrec, xsel in ((0, yrec0, x0), (1, yrec1, x1)):
         wait_for(yrec.at[pl.ds(0, NY - 1)], gsend.at[3 * w + 1])
         for _ in range(NX - 1):
             wait_for(xsel, gsend.at[3 * w + 2])
@@ -344,7 +386,6 @@
     naux, rows, width = three_index.shape
     factor = float(naux * fock_count * occ_coef.shape[1]) ** (-0.5)
     bf, f32 = jnp.bfloat16, jnp.float32
-    smem = pl.BlockSpec(memory_space=pltpu.SMEM)
     vmem = pl.BlockSpec(memory_space=pltpu.VMEM)
     dma = pltpu.SemaphoreType.DMA
     g = pltpu.VMEM((NZ, 16, CHUNK), bf)
@@ -359,12 +400,18 @@
     return pl.pallas_call(
         body,
         out_shape=jax.ShapeDtypeStruct((16, BS), f32),
-        in_specs=[pl.BlockSpec(memory_space=pl.ANY), smem, smem, vmem, smem, smem],
+        in_specs=[pl.BlockSpec(memory_space=pl.ANY)] * 6,
         out_specs=vmem,
         scratch_shapes=[
+            pltpu.SMEM((SLOTS, NAUX_DEV), jnp.int32),
+            pltpu.SMEM((SLOTS, NAUX_DEV), jnp.int32),
+            pltpu.VMEM(occ_coef.shape, bf),
+            pltpu.SMEM((2 * CHUNKS, NAUX_DEV), jnp.int32),
+            pltpu.SMEM((2, kept.shape[0]), jnp.int32),
+            dma((5,)),
             pltpu.VMEM((NY, NZ, rows, width), bf),
             pltpu.VMEM((CHUNKS, NX, 16, CHUNK), bf),
-            g, g, ysel, ysel, ysel, ysel, xsel, xsel, wt, wt, wt, send, send, send, recv, recv, recv,
+            g, pltpu.VMEM((NZ // 2, 16, CHUNK), bf), ysel, ysel, ysel, ysel, xsel, xsel, wt, wt, wt, wt, send, send, send, recv, recv, recv,
             pltpu.VMEM((NX, NC, 8, NY, 16, 2 * BS), f32),
             pltpu.VMEM((NX, 8, NY, 16, 2 * BS), f32),
             pltpu.VMEM((NX, 8, NY, 16, 2 * BS), f32),
@@ -378,7 +425,7 @@
             pltpu.VMEM((8, 16, 2 * BS), f32),
             pltpu.VMEM((NZ, 8, 2 * BS), f32),
             pltpu.VMEM((NZ, 8, 2 * BS), f32),
-            dma, dma((7,)), dma((7,)), dma((3,)), dma((3,)), dma((4,)), dma((4,)), dma((4,)), dma((4,)),
+            dma, dma((8,)), dma((8,)), dma((3,)), dma((3,)), dma((4,)), dma((4,)), dma((4,)), dma((4,)),
             dma((7,)), dma((7,)),
         ],
         compiler_params=pltpu.CompilerParams(

time: 192 us -> 188 us (0.979)
  Pallas kernels: 190 us -> 186 us
    pallas_call x1, Pallas kernels: 190 us -> 186 us  [per_device(): pl.pallas_call(body, out_shape=jax.ShapeDtypeStruct((16, BS), f32), in_sp...]
where the time goes in v3:
time: 188 us
  Pallas kernels  186 us (99%)
    pallas_call x1, Pallas kernels, per_device(): pl.pallas_call(body, out_shape=jax.ShapeDtypeStruct((16, BS), f32), in_sp...  186 us

profile of v3, /device:TPU:1, one launch (start us, length us, event | category | flops | bytes accessed | tf_op | source)
XLA Modules:
  0.0 187.7 jit_solution(11800780786110598571)
XLA Ops:
  0.0 186.4 %shard_map.64 = f32[16,64]{1,0:T(8,128)} custom-call(bf16[4,16,64,512]{3,2,1,0:T(8,128)(2,1)} %bitcast.5, s32[8,64]{1,0:T(8,128)} %bitcast.6, s32[8,64]{1,0:T(8,128)} %bitcast.7, bf16[64,384]{1,0:T(8,128)(2,1)} %refs_3_.1, s32[6,64]{1,0:T(8,128)} %bitcast.8, s32[2,128]{1,0:T(2,128)} %bitcast.9), custom_call_target="tpu_custom_call" | custom-call | flops 2400000000 | bytes 8000000 | tf_op jit(solution)/shard_map/pallas_call | solution.py:400
  186.4 1.3 copy.8

commit v4 on v3

--- a/solution.py
+++ b/solution.py
@@ -18,7 +18,7 @@
     pltpu.make_async_copy(ref, ref, sem).wait()
 
 
-def kernel(factor, three_ref, colb_hbm, pmask_hbm, coef_hbm, omask_hbm, kept_hbm, out_ref,
+def kernel(three_ref, colb_hbm, pmask_hbm, coef_hbm, omask_hbm, kept_hbm, out_ref,
            colb_ref, pmask_ref, coef_ref, omask_ref, kept_ref, isem, tri, masked, g0, g1, ysel0, ysel1, yrec0, yrec1, x0, x1, w0, w1, w2, w3, s0, s1, s2, r0, r1, r2,
            kacc, cb, xs, xb, ys, yb, early, kst, cb2, a1s, a1r, b1s, b1r, a2s, a2r, b2s, b2r, vb, zs, zb,
            tsem, gsend, grecv, asend, arecv, csend, crecv, c2send, c2recv, tsend, trecv):
@@ -353,7 +353,7 @@
     lax.fori_loop(1, NZ, z_send, 0)
     zb[z] = zs[z]
     wait_for(zb.at[pl.ds(0, NZ - 1)], trecv.at[6])
-    result = jnp.sum(zb[...], axis=0) * factor
+    result = jnp.sum(zb[...], axis=0)
     out_ref[0:8, :] = result[:, :BS]
     out_ref[8:16, :] = result[:, BS:]
 
@@ -396,9 +396,8 @@
     recv = pltpu.VMEM((NAUX_DEV, BS, CHUNK), bf)
     first = pltpu.VMEM((4, 4, 4, 16, 2 * BS), bf)
     second = pltpu.VMEM((4, 4, 16, 2 * BS), bf)
-    body = lambda *refs: kernel(factor, *refs)
-    return pl.pallas_call(
-        body,
+    total = pl.pallas_call(
+        kernel,
         out_shape=jax.ShapeDtypeStruct((16, BS), f32),
         in_specs=[pl.BlockSpec(memory_space=pl.ANY)] * 6,
         out_specs=vmem,
@@ -432,6 +431,7 @@
             collective_id=0, has_side_effects=True, vmem_limit_bytes=62 * 2**20),
         cost_estimate=pl.CostEstimate(flops=2_400_000_000, bytes_accessed=8_000_000, transcendentals=0),
     )(three_index.reshape(NY, NZ, rows, width), col_blocks.T, pair_mask.T, occ_coef, occ_mask.T, kept.T)
+    return total * factor
 
 
 def solution(mesh):

time: 188 us -> 188 us (level)
  no operation moved by 1% of the time
where the time goes in v4:
time: 188 us
  Pallas kernels  186 us (99%)
    pallas_call x1, Pallas kernels, per_device(): pl.pallas_call(kernel, out_shape=jax.ShapeDtypeStruct((16, BS), f32), in_...  186 us

profile of v4, /device:TPU:1, one launch (start us, length us, event | category | flops | bytes accessed | tf_op | source)
XLA Modules:
  0.0 187.7 jit_solution(265064517583771524)
XLA Ops:
  0.0 186.4 %shard_map.64 = f32[16,64]{1,0:T(8,128)} custom-call(bf16[4,16,64,512]{3,2,1,0:T(8,128)(2,1)} %bitcast.5, s32[8,64]{1,0:T(8,128)} %bitcast.6, s32[8,64]{1,0:T(8,128)} %bitcast.7, bf16[64,384]{1,0:T(8,128)(2,1)} %coef_hbm.1, s32[6,64]{1,0:T(8,128)} %bitcast.8, s32[2,128]{1,0:T(2,128)} %bitcast.9), custom_call_target="tpu_custom_call" | custom-call | flops 2400000000 | bytes 8000000 | tf_op jit(solution)/shard_map/pallas_call | solution.py:399
  186.4 1.3 broadcast_multiply_fusion
